TPU v7x, 128 devices: a whole 4x4x4 slice. The times are simulated.
128 devices in a mesh: section: 16 (over z_lo, y, core), tensor: 8 (over z_hi, x).
Axes of the slice: x: 4, y: 4, z: 4 (z_hi: 2, z_lo: 2; z = z_hi * 2 + z_lo), core: 2. Of those that a mesh axis runs over, the one named last changes fastest.
Arguments:
- inputs_down: bfloat16 [16, 2, 240, 2048], P('section', None, 'tensor'), may hold values from -6 to 6
- inputs_up: bfloat16 [16, 2, 240, 2048], P('section', None, 'tensor'), may hold values from -6 to 6
- grads_down: bfloat16 [16, 240, 2048], P('section', 'tensor'), may hold values from -6 to 6
- grads_up: bfloat16 [16, 240, 2048], P('section', 'tensor'), may hold values from -6 to 6
- loss_grads: bfloat16 [2, 240, 2048], P(None, 'tensor'), may hold values from -6 to 6
- first_down: bfloat16 [16, 2048, 4096], P('section', None, 'tensor'), may hold values from -6 to 6
- second_down: bfloat16 [16, 4096, 2048], P('section', 'tensor'), may hold values from -6 to 6
- first_up: bfloat16 [16, 2048, 4096], P('section', None, 'tensor'), may hold values from -6 to 6
- second_up: bfloat16 [16, 4096, 2048], P('section', 'tensor'), may hold values from -6 to 6
- momentum_first: bfloat16 [16, 2048, 4096], P('section', None, 'tensor'), may hold values from -3 to 3
- momentum_second: bfloat16 [16, 4096, 2048], P('section', 'tensor'), may hold values from -3 to 3
Outputs:
- first_new: bfloat16 [16, 2048, 4096], P('section', None, 'tensor')
- second_new: bfloat16 [16, 4096, 2048], P('section', 'tensor')
- momentum_one: bfloat16 [16, 2048, 4096], P('section', None, 'tensor')
- momentum_two: bfloat16 [16, 4096, 2048], P('section', 'tensor')
- passed_down: bfloat16 [16, 240, 2048], P('section', 'tensor')
- passed_up: bfloat16 [16, 240, 2048], P('section', 'tensor')
All inputs are finite; a program needn't handle non-finite values.
Results may differ from a plain program's by a relative error of at most 0.0063.
Values may be sent and summed in bfloat16 or wider, within the bound.
A program may use at most 128 MiB of HBM per device.

v0:
```python
import jax
import jax.numpy as jnp
from jax import lax
from jax.sharding import PartitionSpec as P

D = 2048
FF = 4096
epsilon = 1e-05
learning_rate = 0.25
momentum_decay = 0.9
tanh_scale = 0.7978845608028654
cubic_term = 0.044715


def passed_along(value, axis, by):
    devices = lax.axis_size(axis)
    pairs = [(i, i + by) for i in range(devices) if 0 <= i + by < devices]
    return lax.ppermute(value, axis, pairs)


def partner(value, axis, bit):
    mask = 2**bit
    pairs = [(source, source ^ mask) for source in range(lax.axis_size(axis))]
    return lax.ppermute(value, axis, pairs)


def gelu_with_slope(preact):
    tanh_input = tanh_scale * (preact + cubic_term * preact * preact * preact)
    tangent = jnp.tanh(tanh_input)
    values = 0.5 * preact * (1.0 + tangent)
    slopes = 0.5 * (1.0 + tangent) + 0.5 * preact * (1.0 - tangent * tangent) * tanh_scale * (
        1.0 + 3.0 * cubic_term * preact * preact
    )
    return (values, slopes)


def normalize(inputs):
    widened = inputs.astype(jnp.float32)
    centred = widened - jnp.mean(widened, axis=-1, keepdims=True)
    inverse_scale = lax.rsqrt(jnp.mean(centred * centred, axis=-1, keepdims=True) + epsilon)
    return (centred * inverse_scale, inverse_scale)


def contract_rows(left_side, right_side):
    return lax.dot_general(
        left_side, right_side, (((0,), (0,)), ((), ())), preferred_element_type=jnp.float32
    )


def contract_last(left_side, right_side):
    return lax.dot_general(
        left_side, right_side, (((1,), (1,)), ((), ())), preferred_element_type=jnp.float32
    )


def body(
    inputs_down,
    inputs_up,
    grads_down,
    grads_up,
    loss_grads,
    first_down,
    second_down,
    first_up,
    second_up,
    momentum_first,
    momentum_second,
):
    section_count = lax.axis_size("section")
    position = lax.axis_index("section")
    row_count = grads_down.shape[1]
    row_start = lax.axis_index("tensor") * row_count
    model_width = first_down.shape[1]
    hidden_local = first_down.shape[2]
    firsts = (first_down[0], first_up[0])
    seconds = (second_down[0], second_up[0])
    cotans = (grads_down[0], grads_up[0])
    kept_cotans = []
    records = []
    passed = []
    for step_index in range(2):
        gathered = (
            lax.all_gather(inputs_down[0, step_index], "tensor", axis=0, tiled=True),
            lax.all_gather(inputs_up[0, step_index], "tensor", axis=0, tiled=True),
            lax.all_gather(cotans[0], "tensor", axis=0, tiled=True),
            lax.all_gather(cotans[1], "tensor", axis=0, tiled=True),
        )
        results = []
        for branch in range(2):
            normed, inverse_scale = normalize(gathered[branch])
            normed_low = normed.astype(jnp.bfloat16)
            preact = jnp.dot(
                normed_low, firsts[branch], preferred_element_type=jnp.float32
            ) * D ** (-0.5)
            values, slopes = gelu_with_slope(preact)
            activation = values.astype(jnp.bfloat16)
            grad_activation = contract_last(gathered[2 + branch], seconds[branch]) * FF ** (-0.5)
            grad_preact = (grad_activation * slopes).astype(jnp.bfloat16)
            results.append(
                (normed, inverse_scale, normed_low, activation, grad_preact, gathered[2 + branch])
            )
        pieces = []
        for hidden_branch in range(2):
            row_piece = results[hidden_branch][4]
            pieces.append(contract_last(row_piece, firsts[hidden_branch]) * D ** (-0.5))
        grad_normed_both = lax.psum_scatter(
            jnp.concatenate(pieces, axis=1), "tensor", scatter_dimension=0, tiled=True
        )
        passed = []
        for branch in range(2):
            own_normed = lax.dynamic_slice_in_dim(results[branch][0], row_start, row_count, 0)
            own_scale = lax.dynamic_slice_in_dim(results[branch][1], row_start, row_count, 0)
            grad_normed = grad_normed_both[:, branch * model_width : (branch + 1) * model_width]
            first_mean = jnp.mean(grad_normed, axis=-1, keepdims=True)
            second_mean = jnp.mean(grad_normed * own_normed, axis=-1, keepdims=True)
            grad_inputs = cotans[branch].astype(jnp.float32) + own_scale * (
                grad_normed - first_mean - own_normed * second_mean
            )
            passed.append(grad_inputs.astype(jnp.bfloat16))
        records.append(results)
        kept_cotans.append(cotans)
        if step_index == 0:
            from_above = passed_along(passed[0], "section", -1)
            from_below = passed_along(passed[1], "section", 1)
            cotans = (
                jnp.where(position == section_count - 1, loss_grads[0], from_above),
                jnp.where(position == 0, loss_grads[1], from_below),
            )

    def joined(branch, item):
        return jnp.concatenate([records[0][branch][item], records[1][branch][item]], axis=0)

    down_first = contract_rows(joined(0, 2), joined(0, 4)) * D ** (-0.5)
    down_second = contract_rows(joined(0, 3), joined(0, 5)) * FF ** (-0.5)
    bit_total = section_count.bit_length() - 1
    up_first = contract_rows(joined(1, 2), joined(1, 4)) * D ** (-0.5)
    up_second = contract_rows(joined(1, 3), joined(1, 5)) * FF ** (-0.5)
    payload = jnp.concatenate(
        [up_first.astype(jnp.bfloat16).reshape(-1), up_second.astype(jnp.bfloat16).reshape(-1)]
    )
    for bit_index in range(bit_total):
        payload = partner(payload, "section", bit_index)
    size_one = model_width * hidden_local
    mirror_first = payload[:size_one].reshape(model_width, hidden_local)
    mirror_second = payload[size_one:].reshape(hidden_local, model_width)
    total_first = down_first + mirror_first.astype(jnp.float32)
    total_second = down_second + mirror_second.astype(jnp.float32)
    moment_first = momentum_decay * momentum_first[0].astype(jnp.float32) + total_first
    moment_second = momentum_decay * momentum_second[0].astype(jnp.float32) + total_second
    first_new = (first_down[0].astype(jnp.float32) - learning_rate * moment_first).astype(
        jnp.bfloat16
    )
    second_new = (second_down[0].astype(jnp.float32) - learning_rate * moment_second).astype(
        jnp.bfloat16
    )
    return (
        first_new[None],
        second_new[None],
        moment_first.astype(jnp.bfloat16)[None],
        moment_second.astype(jnp.bfloat16)[None],
        passed[0][None],
        passed[1][None],
    )


def solution(mesh):
    placed = (
        P("section", None, "tensor", None),
        P("section", None, "tensor", None),
        P("section", "tensor", None),
        P("section", "tensor", None),
        P(None, "tensor", None),
        P("section", None, "tensor"),
        P("section", "tensor", None),
        P("section", None, "tensor"),
        P("section", "tensor", None),
        P("section", None, "tensor"),
        P("section", "tensor", None),
    )
    return jax.shard_map(
        body,
        mesh=mesh,
        in_specs=placed,
        out_specs=(
            P("section", None, "tensor"),
            P("section", "tensor", None),
            P("section", None, "tensor"),
            P("section", "tensor", None),
            P("section", "tensor", None),
            P("section", "tensor", None),
        ),
        check_vma=False,
    )
```

profile of v0, /device:TPU:8, one launch (start us, length us, event | category | flops | bytes accessed | tf_op | source)
XLA Modules:
  0.0 823.8 jit_solution(11953718026809434699)
XLA Ops:
  8.9 39.4 %all-gather.4 = bf16[1,1,240,2048]{3,1,0,2:T(2,128)(2,1)S(1)} all-gather(bf16[1,1,30,2048]{3,1,0,2:T(2,128)(2,1)S(1)} %get-tuple-element.37), channel_id=6, replica_groups=mesh['section'=16,'tensor'=8] {'tensor'}, dimensions={2}, use_global_device_ids=true | all-gather | bytes 1105920 | tf_op jit(solution)/shard_map/all_gather | solution.py:84
  53.2 38.7 %all-gather = bf16[1,1,240,2048]{3,1,0,2:T(2,128)(2,1)S(1)} all-gather(bf16[1,1,30,2048]{3,1,0,2:T(2,128)(2,1)S(1)} %get-tuple-element.35), channel_id=2, replica_groups=mesh['section'=16,'tensor'=8] {'tensor'}, dimensions={2}, use_global_device_ids=true | all-gather | bytes 1105920 | tf_op jit(solution)/shard_map/all_gather | solution.py:83
  98.7 39.1 %all-gather.3 = bf16[1,240,2048]{2,0,1:T(2,128)(2,1)S(1)} all-gather(bf16[1,30,2048]{2,0,1:T(2,128)(2,1)S(1)} %copy.44), channel_id=5, replica_groups=mesh['section'=16,'tensor'=8] {'tensor'}, dimensions={1}, use_global_device_ids=true | all-gather | bytes 1105920 | tf_op jit(solution)/shard_map/all_gather | solution.py:86
  145.1 37.9 %all-gather.2 = bf16[1,240,2048]{2,0,1:T(2,128)(2,1)S(1)} all-gather(bf16[1,30,2048]{2,0,1:T(2,128)(2,1)S(1)} %copy.42), channel_id=4, replica_groups=mesh['section'=16,'tensor'=8] {'tensor'}, dimensions={1}, use_global_device_ids=true | all-gather | bytes 1105920 | tf_op jit(solution)/shard_map/all_gather | solution.py:85
  191.4 45.2 %all-gather.5 = bf16[1,1,240,2048]{3,1,0,2:T(2,128)(2,1)S(1)} all-gather(bf16[1,1,30,2048]{3,1,0,2:T(2,128)(2,1)S(1)} %get-tuple-element.36), channel_id=7, replica_groups=mesh['section'=16,'tensor'=8] {'tensor'}, dimensions={2}, use_global_device_ids=true | all-gather | bytes 1105920 | tf_op jit(solution)/shard_map/all_gather | solution.py:84
  240.5 62.5 %all-reduce.5.cloned.1.call-done = f32[240,4096]{1,0:T(8,128)} async-done(((f32[240,4096]{1,0:T(8,128)}), f32[240,4096]{1,0:T(8,128)}) %all-reduce.5.cloned.1.call-update) | async-done | bytes 3932176
  310.3 2.8 collective-permute-done.1
  313.1 48.0 %all-gather.7 = bf16[8,30,2048]{2,1,0:T(8,128)(2,1)S(1)} all-gather(bf16[1,30,2048]{2,1,0:T(8,128)(2,1)S(1)} %fusion.123), channel_id=1, replica_groups=mesh['section'=16,'tensor'=8] {'tensor'}, dimensions={0}, use_global_device_ids=true | all-gather | bytes 1105920 | tf_op jit(solution)/shard_map/all_gather | solution.py:86
  362.4 3.1 fusion.76
  371.0 14.6 %pad_maximum_fusion = bf16[2097152]{0:T(1024)(128)(2,1)S(1)} fusion(bf16[1048576]{0:T(1024)(128)(2,1)S(1)} %bitcast.178, bf16[1048576]{0:T(1024)(128)(2,1)S(1)} %bitcast.177), kind=kLoop, calls=%fused_computation | loop fusion | flops 8388608 | bytes 8388608 | tf_op jit(solution)/shard_map/concatenate | solution.py:138
  385.7 7.1 collective-permute-done.2
  392.9 39.1 %all-gather.1 = bf16[1,1,240,2048]{3,1,0,2:T(2,128)(2,1)S(1)} all-gather(bf16[1,1,30,2048]{3,1,0,2:T(2,128)(2,1)S(1)} %copy-done.25), channel_id=3, replica_groups=mesh['section'=16,'tensor'=8] {'tensor'}, dimensions={2}, use_global_device_ids=true | all-gather | bytes 1105920 | tf_op jit(solution)/shard_map/all_gather | solution.py:83
  433.2 52.4 %collective-permute-done.3 = bf16[2097152]{0:T(1024)(128)(2,1)} collective-permute-done((bf16[2097152]{0:T(1024)(128)(2,1)S(1)}, bf16[2097152]{0:T(1024)(128)(2,1)}, u32[]{:S(2)}, u32[]{:S(2)}) %collective-permute-start.3) | collective-permute-done | bytes 4194336 | tf_op jit(solution)/shard_map/ppermute | solution.py:24
  493.2 85.3 %collective-permute-done = bf16[30,2048]{1,0:T(8,128)(2,1)S(1)} collective-permute-done((bf16[30,2048]{1,0:T(8,128)(2,1)S(1)}, bf16[30,2048]{1,0:T(8,128)(2,1)S(1)}, u32[]{:S(2)}, u32[]{:S(2)}) %collective-permute-start) | collective-permute-done | bytes 122912 | tf_op jit(solution)/shard_map/ppermute | solution.py:18
  579.3 36.7 %all-gather.6 = bf16[8,30,2048]{2,1,0:T(8,128)(2,1)S(1)} all-gather(bf16[1,30,2048]{2,1,0:T(8,128)(2,1)S(1)} %fusion.122), channel_id=1, replica_groups=mesh['section'=16,'tensor'=8] {'tensor'}, dimensions={0}, use_global_device_ids=true | all-gather | bytes 1105920 | tf_op jit(solution)/shard_map/all_gather | solution.py:85
  625.2 5.0 fusion.30
  630.2 3.2 fusion.40
  633.4 97.3 %all-reduce.7.cloned.1.call-done = f32[240,4096]{1,0:T(8,128)} async-done(((f32[240,4096]{1,0:T(8,128)}), f32[240,4096]{1,0:T(8,128)}) %all-reduce.7.cloned.1.call-update) | async-done | bytes 3932176
  734.6 52.7 %collective-permute-done.5 = bf16[2097152]{0:T(1024)(128)(2,1)} collective-permute-done((bf16[2097152]{0:T(1024)(128)(2,1)}, bf16[2097152]{0:T(1024)(128)(2,1)}, u32[]{:S(2)}, u32[]{:S(2)}) %collective-permute-start.5) | collective-permute-done | bytes 4194336 | tf_op jit(solution)/shard_map/ppermute | solution.py:24
  787.4 6.0 slice_convert_fusion
  793.4 4.9 reshape.189
  798.3 4.9 reshape.188
  803.2 8.7 %convert_bitcast_fusion.2 = (bf16[1,512,2048]{2,1,0:T(8,128)(2,1)}, bf16[1,512,2048]{2,1,0:T(8,128)(2,1)}) fusion(f32[512,2048]{1,0:T(8,128)} %reshape.189, f32[512,2048]{1,0:T(8,128)} %fusion.40, bf16[1,512,2048]{2,1,0:T(8,128)(2,1)} %param.21, bf16[1,512,2048]{2,1,0:T(8,128)(2,1)} %param.17), kind=kLoop, calls=%fused_computation.41 | loop fusion | flops 10485760 | bytes 16777216 | tf_op jit(solution)/shard_map/broadcast_in_dim | solution.py:160
  813.0 3.6 convert_bitcast_fusion.3
  (160 shorter events, 70.0 us)
Async XLA Ops:
  7.2 131.3 %copy-start = (bf16[1,2048,512]{2,1,0:T(8,128)(2,1)S(1)}, bf16[1,2048,512]{2,1,0:T(8,128)(2,1)}, u32[]{:S(2)}) copy-start(bf16[1,2048,512]{2,1,0:T(8,128)(2,1)} %param.18) | copy-start | bytes 6291460
  7.2 295.8 %all-reduce.5.cloned.1.call-start = ((), (), s32[]{:S(2)}) async-start(), calls=%async_computation | async-start | bytes 7864320
  98.5 39.9 %copy-start.17 = (bf16[240,2048]{1,0:T(8,128)(2,1)}, bf16[240,2048]{1,0:T(8,128)(2,1)S(1)}, u32[]{:S(2)}) copy-start(bf16[240,2048]{1,0:T(8,128)(2,1)S(1)} %get-tuple-element.20) | copy-start | bytes 2949124
  144.9 38.6 %copy-start.14 = (bf16[240,2048]{1,0:T(8,128)(2,1)}, bf16[240,2048]{1,0:T(8,128)(2,1)S(1)}, u32[]{:S(2)}) copy-start(bf16[240,2048]{1,0:T(8,128)(2,1)S(1)} %get-tuple-element.18) | copy-start | bytes 2949124
  145.1 38.5 %copy-start.1 = (bf16[1,2048,512]{2,1,0:T(8,128)(2,1)S(1)}, bf16[1,2048,512]{2,1,0:T(8,128)(2,1)}, u32[]{:S(2)}) copy-start(bf16[1,2048,512]{2,1,0:T(8,128)(2,1)} %param.16) | copy-start | bytes 6291460
  189.5 541.2 %all-reduce.7.cloned.1.call-start = ((), (), s32[]{:S(2)}) async-start(), calls=%async_computation.1 | async-start | bytes 7864320
  238.2 74.9 %copy-start.10 = (bf16[1,30,2048]{2,0,1:T(2,128)(2,1)}, bf16[1,30,2048]{2,0,1:T(2,128)(2,1)S(1)}, u32[]{:S(2)}) copy-start(bf16[1,30,2048]{2,0,1:T(2,128)(2,1)S(1)} %get-tuple-element.33) | copy-start | bytes 368644
  303.0 5.7 copy-start.19
  306.8 6.3 collective-permute-start.1
  371.0 21.9 %copy-start.25 = (bf16[1,1,30,2048]{3,1,0,2:T(2,128)(2,1)S(1)}, bf16[1,1,30,2048]{3,1,0,2:T(2,128)(2,1)}, u32[]{:S(2)}) copy-start(bf16[1,1,30,2048]{3,1,0,2:T(2,128)(2,1)} %get-tuple-element.34) | copy-start | bytes 368644
  385.6 7.2 collective-permute-start.2
  392.9 92.7 %collective-permute-start.3 = (bf16[2097152]{0:T(1024)(128)(2,1)S(1)}, bf16[2097152]{0:T(1024)(128)(2,1)}, u32[]{:S(2)}, u32[]{:S(2)}) collective-permute-start(bf16[2097152]{0:T(1024)(128)(2,1)S(1)} %collective-permute-done.2), channel_id=1, source_target_pairs={{0,16},{8,24},{16,0},{24,8},{32,48},{40,56},{48,32},{56,40},{64,80... | collective-permute-start | bytes 12582920 | tf_op jit(solution)/shard_map/ppermute | solution.py:24
  433.2 56.5 %copy-start.36 = (bf16[30,2048]{1,0:T(8,128)(2,1)S(1)}, bf16[30,2048]{1,0:T(8,128)(2,1)}, u32[]{:S(2)}) copy-start(bf16[30,2048]{1,0:T(8,128)(2,1)} %get-tuple-element.30) | copy-start | bytes 368644
  433.2 58.4 %copy-start.2 = (bf16[1,2048,512]{2,1,0:T(8,128)(2,1)S(1)}, bf16[1,2048,512]{2,1,0:T(8,128)(2,1)}, u32[]{:S(2)}) copy-start(bf16[1,2048,512]{2,1,0:T(8,128)(2,1)} %param.16) | copy-start | bytes 6291460
  485.6 138.3 %collective-permute-start.4 = (bf16[2097152]{0:T(1024)(128)(2,1)}, bf16[2097152]{0:T(1024)(128)(2,1)}, u32[]{:S(2)}, u32[]{:S(2)}) collective-permute-start(bf16[2097152]{0:T(1024)(128)(2,1)} %collective-permute-done.3), channel_id=1, source_target_pairs={{0,32},{8,40},{16,48},{24,56},{32,0},{40,8},{48,16},{56,24},{64,96... | collective-permute-start | bytes 12582920 | tf_op jit(solution)/shard_map/ppermute | solution.py:24
  489.6 88.9 %collective-permute-start = (bf16[30,2048]{1,0:T(8,128)(2,1)S(1)}, bf16[30,2048]{1,0:T(8,128)(2,1)S(1)}, u32[]{:S(2)}, u32[]{:S(2)}) collective-permute-start(bf16[30,2048]{1,0:T(8,128)(2,1)S(1)} %copy-done.36), channel_id=1, source_target_pairs={{8,0},{16,8},{24,16},{32,24},{40,32},{48,40},{56,48},{64,56},{72,6... | collective-permute-start | bytes 368648 | tf_op jit(solution)/shard_map/ppermute | solution.py:18
  623.9 163.5 %collective-permute-start.5 = (bf16[2097152]{0:T(1024)(128)(2,1)}, bf16[2097152]{0:T(1024)(128)(2,1)}, u32[]{:S(2)}, u32[]{:S(2)}) collective-permute-start(bf16[2097152]{0:T(1024)(128)(2,1)} %collective-permute-done.4), channel_id=1, source_target_pairs={{0,64},{8,72},{16,80},{24,88},{32,96},{40,104},{48,112},{56,120},{... | collective-permute-start | bytes 12582920 | tf_op jit(solution)/shard_map/ppermute | solution.py:24
  625.2 5.0 copy-start.8
  625.2 5.0 copy-start.29
  625.2 5.0 copy-start.34
  803.2 8.7 %copy-start.4 = (bf16[1,2048,512]{2,1,0:T(8,128)(2,1)S(1)}, bf16[1,2048,512]{2,1,0:T(8,128)(2,1)}, u32[]{:S(2)}) copy-start(bf16[1,2048,512]{2,1,0:T(8,128)(2,1)} %param.16) | copy-start | bytes 6291460
  803.2 8.7 %copy-start.5 = (f32[2048,512]{1,0:T(8,128)S(1)}, f32[2048,512]{1,0:T(8,128)}, u32[]{:S(2)}) copy-start(f32[2048,512]{1,0:T(8,128)} %reshape.188) | copy-start | bytes 12582916
  803.2 8.7 %copy-start.6 = (f32[2048,512]{1,0:T(8,128)S(1)}, f32[2048,512]{1,0:T(8,128)}, u32[]{:S(2)}) copy-start(f32[2048,512]{1,0:T(8,128)} %fusion.30) | copy-start | bytes 12582916
  803.2 9.8 %copy-start.13 = (bf16[1,2048,512]{2,1,0:T(8,128)(2,1)S(1)}, bf16[1,2048,512]{2,1,0:T(8,128)(2,1)}, u32[]{:S(2)}) copy-start(bf16[1,2048,512]{2,1,0:T(8,128)(2,1)} %param.20) | copy-start | bytes 6291460
  (26 other events, 47.2 us)
Sparse Core Ops, SparseCore 0:
  189.6 113.3 all-reduce.4
  624.0 106.6 all-reduce.6
where the time goes:
time: 832 us; the launch traced here: 824 us
  waiting for transfers between devices  360 us (43%)
  blocking collectives  324 us (39%)
  other arithmetic  64.9 us (8%)
  matrix products  27.1 us (3%)
  local copies, waits for them, and re-layouts  24.7 us (3%)
  between operations  15.6 us (2%)
    unnamed x4, waiting for transfers between devices  160 us
    ppermute x4, waiting for transfers between devices, partner(): return lax.ppermute(value, axis, pairs)  112 us
    ppermute x2, waiting for transfers between devices, passed_along(): return lax.ppermute(value, axis, pairs)  88.1 us
    all_gather x2, blocking collectives, body(): lax.all_gather(cotans[1], 'tensor', axis=0, tiled=True)  87.2 us
    all_gather x2, blocking collectives, body(): lax.all_gather(inputs_up[0, step_index], 'tensor', axis=0, tiled=True)  84.6 us
    all_gather x2, blocking collectives, body(): lax.all_gather(inputs_down[0, step_index], 'tensor', axis=0, tiled=True)  77.8 us
    all_gather x2, blocking collectives, body(): lax.all_gather(cotans[0], 'tensor', axis=0, tiled=True)  74.5 us
  transfers between devices with their start and end apart: 8, of which 7 were waited for; matrix products, arithmetic and copies ran while one was open for 4% of the time, Pallas kernels for 0%

commit v1 on v0

--- a/solution.py
+++ b/solution.py
@@ -83,7 +83,10 @@
             lax.all_gather(inputs_down[0, step_index], "tensor", axis=0, tiled=True),
             lax.all_gather(inputs_up[0, step_index], "tensor", axis=0, tiled=True),
             lax.all_gather(cotans[0], "tensor", axis=0, tiled=True),
-            lax.all_gather(cotans[1], "tensor", axis=0, tiled=True),
+            jnp.concatenate(
+                lax.all_to_all(jnp.stack([cotans[1]] * lax.axis_size("tensor")), "tensor", 0, 0),
+                axis=0,
+            ),
         )
         results = []
         for branch in range(2):

time: 832 us -> 785 us (0.944)
  blocking collectives: 324 us -> 245 us
  waiting for transfers between devices: 360 us -> 373 us
  starting transfers between devices: 7.23 us -> 18.3 us
    all_gather x2 -> x0, blocking collectives: 87.2 us -> none  [body(): lax.all_gather(cotans[1], 'tensor', axis=0, tiled=True)]
    all_to_all x0 -> x2, starting transfers between devices: none -> 12.1 us  [body(): lax.all_to_all(jnp.stack([cotans[1]] * lax.axis_size('tensor')), 'tensor'...]
    all_to_all x0 -> x2, waiting for transfers between devices: none -> 10.2 us  [body(): lax.all_to_all(jnp.stack([cotans[1]] * lax.axis_size('tensor')), 'tensor'...]
  transfers between devices with their start and end apart: 8 -> 10, of which waited for: 7 -> 8; matrix products, arithmetic and copies ran while one was open for 4% -> 7% of each run, Pallas kernels for 0% -> 0%
where the time goes in v1:
time: 785 us; the launch traced here: 780 us
  waiting for transfers between devices  373 us (48%)
  blocking collectives  245 us (31%)
  other arithmetic  66.4 us (8%)
  matrix products  31.2 us (4%)
  local copies, waits for them, and re-layouts  30.8 us (4%)
  starting transfers between devices  18.3 us (2%)
  between operations  15.4 us (2%)
    unnamed x4, waiting for transfers between devices  158 us
    ppermute x4, waiting for transfers between devices, partner(): return lax.ppermute(value, axis, pairs)  115 us
    all_gather x2, blocking collectives, body(): lax.all_gather(inputs_up[0, step_index], 'tensor', axis=0, tiled=True)  91.8 us
    ppermute x2, waiting for transfers between devices, passed_along(): return lax.ppermute(value, axis, pairs)  89.6 us
    all_gather x2, blocking collectives, body(): lax.all_gather(inputs_down[0, step_index], 'tensor', axis=0, tiled=True)  78.1 us
    all_gather x2, blocking collectives, body(): lax.all_gather(cotans[0], 'tensor', axis=0, tiled=True)  74.8 us
  transfers between devices with their start and end apart: 10, of which 8 were waited for; matrix products, arithmetic and copies ran while one was open for 7% of the time, Pallas kernels for 0%

profile of v1, /device:TPU:8, one launch (start us, length us, event | category | flops | bytes accessed | tf_op | source)
XLA Modules:
  0.0 779.7 jit_solution(15697188359432566574)
XLA Ops:
  9.4 7.6 all-to-all-start
  18.1 48.1 %all-gather.3 = bf16[1,1,240,2048]{3,1,0,2:T(2,128)(2,1)S(1)} all-gather(bf16[1,1,30,2048]{3,1,0,2:T(2,128)(2,1)S(1)} %get-tuple-element.37), channel_id=5, replica_groups=mesh['section'=16,'tensor'=8] {'tensor'}, dimensions={2}, use_global_device_ids=true | all-gather | bytes 1105920 | tf_op jit(solution)/shard_map/all_gather | solution.py:84
  71.1 39.1 %all-gather = bf16[1,1,240,2048]{3,1,0,2:T(2,128)(2,1)S(1)} all-gather(bf16[1,1,30,2048]{3,1,0,2:T(2,128)(2,1)S(1)} %get-tuple-element.35), channel_id=2, replica_groups=mesh['section'=16,'tensor'=8] {'tensor'}, dimensions={2}, use_global_device_ids=true | all-gather | bytes 1105920 | tf_op jit(solution)/shard_map/all_gather | solution.py:83
  119.7 38.0 %all-gather.2 = bf16[1,240,2048]{2,0,1:T(2,128)(2,1)S(1)} all-gather(bf16[1,30,2048]{2,0,1:T(2,128)(2,1)S(1)} %copy.41), channel_id=4, replica_groups=mesh['section'=16,'tensor'=8] {'tensor'}, dimensions={1}, use_global_device_ids=true | all-gather | bytes 1105920 | tf_op jit(solution)/shard_map/all_gather | solution.py:85
  175.5 43.7 %all-gather.4 = bf16[1,1,240,2048]{3,1,0,2:T(2,128)(2,1)S(1)} all-gather(bf16[1,1,30,2048]{3,1,0,2:T(2,128)(2,1)S(1)} %copy-done.27), channel_id=6, replica_groups=mesh['section'=16,'tensor'=8] {'tensor'}, dimensions={2}, use_global_device_ids=true | all-gather | bytes 1105920 | tf_op jit(solution)/shard_map/all_gather | solution.py:84
  221.5 63.4 %all-reduce.5.cloned.1.call-done = f32[240,4096]{1,0:T(8,128)} async-done(((f32[240,4096]{1,0:T(8,128)}), f32[240,4096]{1,0:T(8,128)}) %all-reduce.5.cloned.1.call-update) | async-done | bytes 3932176
  290.5 4.3 collective-permute-done.1
  296.0 4.5 all-to-all-start.1
  300.7 3.5 fusion.124
  306.8 10.2 %all-to-all-done.1 = bf16[8,30,2048]{2,1,0:T(8,128)(2,1)S(1)} async-done(((bf16[8,30,2048]{2,1,0:T(8,128)(2,1)}), bf16[8,30,2048]{2,1,0:T(8,128)(2,1)S(1)}, u32[]{:S(2)}, u32[]{:S(2)}) %all-to-all-start.1) | async-done | bytes 983072 | tf_op jit(solution)/shard_map/all_to_all | solution.py:87
  326.8 15.0 %pad_maximum_fusion = bf16[2097152]{0:T(1024)(128)(2,1)S(1)} fusion(bf16[1048576]{0:T(1024)(128)(2,1)S(1)} %bitcast.168, bf16[1048576]{0:T(1024)(128)(2,1)S(1)} %bitcast.167), kind=kLoop, calls=%fused_computation | loop fusion | flops 8388608 | bytes 8388608 | tf_op jit(solution)/shard_map/concatenate | solution.py:141
  342.0 7.1 collective-permute-done.2
  349.1 38.9 %all-gather.1 = bf16[1,1,240,2048]{3,1,0,2:T(2,128)(2,1)S(1)} all-gather(bf16[1,1,30,2048]{3,1,0,2:T(2,128)(2,1)S(1)} %copy-done.26), channel_id=3, replica_groups=mesh['section'=16,'tensor'=8] {'tensor'}, dimensions={2}, use_global_device_ids=true | all-gather | bytes 1105920 | tf_op jit(solution)/shard_map/all_gather | solution.py:83
  389.3 52.5 %collective-permute-done.3 = bf16[2097152]{0:T(1024)(128)(2,1)} collective-permute-done((bf16[2097152]{0:T(1024)(128)(2,1)S(1)}, bf16[2097152]{0:T(1024)(128)(2,1)}, u32[]{:S(2)}, u32[]{:S(2)}) %collective-permute-start.3) | collective-permute-done | bytes 4194336 | tf_op jit(solution)/shard_map/ppermute | solution.py:24
  449.3 85.3 %collective-permute-done = bf16[30,2048]{1,0:T(8,128)(2,1)S(1)} collective-permute-done((bf16[30,2048]{1,0:T(8,128)(2,1)S(1)}, bf16[30,2048]{1,0:T(8,128)(2,1)S(1)}, u32[]{:S(2)}, u32[]{:S(2)}) %collective-permute-start) | collective-permute-done | bytes 122912 | tf_op jit(solution)/shard_map/ppermute | solution.py:18
  535.3 36.8 %all-gather.5 = bf16[8,30,2048]{2,1,0:T(8,128)(2,1)S(1)} all-gather(bf16[1,30,2048]{2,1,0:T(8,128)(2,1)S(1)} %fusion.121), channel_id=1, replica_groups=mesh['section'=16,'tensor'=8] {'tensor'}, dimensions={0}, use_global_device_ids=true | all-gather | bytes 1105920 | tf_op jit(solution)/shard_map/all_gather | solution.py:85
  581.6 4.8 fusion.30
  589.6 95.0 %all-reduce.7.cloned.1.call-done = f32[240,4096]{1,0:T(8,128)} async-done(((f32[240,4096]{1,0:T(8,128)}), f32[240,4096]{1,0:T(8,128)}) %all-reduce.7.cloned.1.call-update) | async-done | bytes 3932176
  688.4 55.0 %collective-permute-done.5 = bf16[2097152]{0:T(1024)(128)(2,1)} collective-permute-done((bf16[2097152]{0:T(1024)(128)(2,1)}, bf16[2097152]{0:T(1024)(128)(2,1)}, u32[]{:S(2)}, u32[]{:S(2)}) %collective-permute-start.5) | collective-permute-done | bytes 4194336 | tf_op jit(solution)/shard_map/ppermute | solution.py:24
  743.4 6.1 slice_convert_fusion
  749.5 4.9 reshape.200
  754.4 4.9 reshape.199
  759.3 8.7 %convert_bitcast_fusion.2 = (bf16[1,512,2048]{2,1,0:T(8,128)(2,1)}, bf16[1,512,2048]{2,1,0:T(8,128)(2,1)}) fusion(f32[512,2048]{1,0:T(8,128)} %reshape.200, f32[512,2048]{1,0:T(8,128)} %fusion.40, bf16[1,512,2048]{2,1,0:T(8,128)(2,1)} %param.21, bf16[1,512,2048]{2,1,0:T(8,128)(2,1)} %param.17), kind=kLoop, calls=%fused_computation.41 | loop fusion | flops 10485760 | bytes 16777216 | tf_op jit(solution)/shard_map/broadcast_in_dim | solution.py:163
  769.1 3.6 convert_bitcast_fusion.3
  (167 shorter events, 83.1 us)
Async XLA Ops:
  7.2 151.1 %copy-start = (bf16[1,2048,512]{2,1,0:T(8,128)(2,1)S(1)}, bf16[1,2048,512]{2,1,0:T(8,128)(2,1)}, u32[]{:S(2)}) copy-start(bf16[1,2048,512]{2,1,0:T(8,128)(2,1)} %param.18) | copy-start | bytes 6291460
  7.2 9.8 %copy-start.23 = (bf16[1,2,30,2048]{3,1,2,0:T(2,128)(2,1)S(1)}, bf16[1,2,30,2048]{3,1,2,0:T(2,128)(2,1)}, u32[]{:S(2)}) copy-start(bf16[1,2,30,2048]{3,1,2,0:T(2,128)(2,1)} %param.12) | copy-start | bytes 737284
  9.4 155.7 %all-to-all-start = ((bf16[8,30,2048]{2,1,0:T(8,128)(2,1)}), bf16[8,30,2048]{2,1,0:T(8,128)(2,1)S(1)}, u32[]{:S(2)}, u32[]{:S(2)}) async-start(bf16[8,30,2048]{2,1,0:T(8,128)(2,1)} %stack.4), calls=%async_computation | async-start | bytes 2097152 | tf_op jit(solution)/shard_map/all_to_all | solution.py:87
  17.0 267.9 %all-reduce.5.cloned.1.call-start = ((), (), s32[]{:S(2)}) async-start(), calls=%async_computation.2 | async-start | bytes 7864320
  116.8 41.4 %copy-start.16 = (bf16[240,2048]{1,0:T(8,128)(2,1)}, bf16[240,2048]{1,0:T(8,128)(2,1)S(1)}, u32[]{:S(2)}) copy-start(bf16[240,2048]{1,0:T(8,128)(2,1)S(1)} %get-tuple-element.20) | copy-start | bytes 2949124
  119.5 40.4 %copy-start.14 = (bf16[240,2048]{1,0:T(8,128)(2,1)}, bf16[240,2048]{1,0:T(8,128)(2,1)S(1)}, u32[]{:S(2)}) copy-start(bf16[240,2048]{1,0:T(8,128)(2,1)S(1)} %get-tuple-element.18) | copy-start | bytes 2949124
  219.8 66.6 %copy-start.28 = (bf16[1,30,2048]{2,1,0:T(8,128)(2,1)S(1)}, bf16[1,30,2048]{2,1,0:T(8,128)(2,1)}, u32[]{:S(2)}) copy-start(bf16[1,30,2048]{2,1,0:T(8,128)(2,1)} %param.14) | copy-start | bytes 368644
  288.5 6.3 collective-permute-start.1
  296.0 21.0 %all-to-all-start.1 = ((bf16[8,30,2048]{2,1,0:T(8,128)(2,1)}), bf16[8,30,2048]{2,1,0:T(8,128)(2,1)S(1)}, u32[]{:S(2)}, u32[]{:S(2)}) async-start(bf16[8,30,2048]{2,1,0:T(8,128)(2,1)} %stack.5), calls=%async_computation.1 | async-start | bytes 2097152 | tf_op jit(solution)/shard_map/all_to_all | solution.py:87
  300.5 384.1 %all-reduce.7.cloned.1.call-start = ((), (), s32[]{:S(2)}) async-start(), calls=%async_computation.3 | async-start | bytes 7864320
  326.8 22.3 %copy-start.26 = (bf16[1,1,30,2048]{3,1,0,2:T(2,128)(2,1)S(1)}, bf16[1,1,30,2048]{3,1,0,2:T(2,128)(2,1)}, u32[]{:S(2)}) copy-start(bf16[1,1,30,2048]{3,1,0,2:T(2,128)(2,1)} %get-tuple-element.34) | copy-start | bytes 368644
  341.9 7.2 collective-permute-start.2
  349.1 92.7 %collective-permute-start.3 = (bf16[2097152]{0:T(1024)(128)(2,1)S(1)}, bf16[2097152]{0:T(1024)(128)(2,1)}, u32[]{:S(2)}, u32[]{:S(2)}) collective-permute-start(bf16[2097152]{0:T(1024)(128)(2,1)S(1)} %collective-permute-done.2), channel_id=1, source_target_pairs={{0,16},{8,24},{16,0},{24,8},{32,48},{40,56},{48,32},{56,40},{64,80... | collective-permute-start | bytes 12582920 | tf_op jit(solution)/shard_map/ppermute | solution.py:24
  389.2 56.4 %copy-start.40 = (bf16[30,2048]{1,0:T(8,128)(2,1)S(1)}, bf16[30,2048]{1,0:T(8,128)(2,1)}, u32[]{:S(2)}) copy-start(bf16[30,2048]{1,0:T(8,128)(2,1)} %get-tuple-element.30) | copy-start | bytes 368644
  389.3 58.4 %copy-start.3 = (bf16[1,2048,512]{2,1,0:T(8,128)(2,1)S(1)}, bf16[1,2048,512]{2,1,0:T(8,128)(2,1)}, u32[]{:S(2)}) copy-start(bf16[1,2048,512]{2,1,0:T(8,128)(2,1)} %param.16) | copy-start | bytes 6291460
  441.8 138.6 %collective-permute-start.4 = (bf16[2097152]{0:T(1024)(128)(2,1)}, bf16[2097152]{0:T(1024)(128)(2,1)}, u32[]{:S(2)}, u32[]{:S(2)}) collective-permute-start(bf16[2097152]{0:T(1024)(128)(2,1)} %collective-permute-done.3), channel_id=1, source_target_pairs={{0,32},{8,40},{16,48},{24,56},{32,0},{40,8},{48,16},{56,24},{64,96... | collective-permute-start | bytes 12582920 | tf_op jit(solution)/shard_map/ppermute | solution.py:24
  445.6 88.9 %collective-permute-start = (bf16[30,2048]{1,0:T(8,128)(2,1)S(1)}, bf16[30,2048]{1,0:T(8,128)(2,1)S(1)}, u32[]{:S(2)}, u32[]{:S(2)}) collective-permute-start(bf16[30,2048]{1,0:T(8,128)(2,1)S(1)} %copy-done.40), channel_id=1, source_target_pairs={{8,0},{16,8},{24,16},{32,24},{40,32},{48,40},{56,48},{64,56},{72,6... | collective-permute-start | bytes 368648 | tf_op jit(solution)/shard_map/ppermute | solution.py:18
  580.4 163.0 %collective-permute-start.5 = (bf16[2097152]{0:T(1024)(128)(2,1)}, bf16[2097152]{0:T(1024)(128)(2,1)}, u32[]{:S(2)}, u32[]{:S(2)}) collective-permute-start(bf16[2097152]{0:T(1024)(128)(2,1)} %collective-permute-done.4), channel_id=1, source_target_pairs={{0,64},{8,72},{16,80},{24,88},{32,96},{40,104},{48,112},{56,120},{... | collective-permute-start | bytes 12582920 | tf_op jit(solution)/shard_map/ppermute | solution.py:24
  581.6 4.8 copy-start.38
  586.4 99.8 %copy-start.31 = (bf16[30,2048]{1,0:T(8,128)(2,1)S(1)}, bf16[30,2048]{1,0:T(8,128)(2,1)}, u32[]{:S(2)}) copy-start(bf16[30,2048]{1,0:T(8,128)(2,1)} %copy-done.30) | copy-start | bytes 368644
  759.3 8.7 %copy-start.5 = (bf16[1,2048,512]{2,1,0:T(8,128)(2,1)S(1)}, bf16[1,2048,512]{2,1,0:T(8,128)(2,1)}, u32[]{:S(2)}) copy-start(bf16[1,2048,512]{2,1,0:T(8,128)(2,1)} %param.16) | copy-start | bytes 6291460
  759.3 8.7 %copy-start.6 = (f32[2048,512]{1,0:T(8,128)S(1)}, f32[2048,512]{1,0:T(8,128)}, u32[]{:S(2)}) copy-start(f32[2048,512]{1,0:T(8,128)} %reshape.199) | copy-start | bytes 12582916
  759.3 8.7 %copy-start.8 = (f32[2048,512]{1,0:T(8,128)S(1)}, f32[2048,512]{1,0:T(8,128)}, u32[]{:S(2)}) copy-start(f32[2048,512]{1,0:T(8,128)} %fusion.30) | copy-start | bytes 12582916
  759.3 9.8 %copy-start.13 = (bf16[1,2048,512]{2,1,0:T(8,128)(2,1)S(1)}, bf16[1,2048,512]{2,1,0:T(8,128)(2,1)}, u32[]{:S(2)}) copy-start(bf16[1,2048,512]{2,1,0:T(8,128)(2,1)} %param.20) | copy-start | bytes 6291460
  (30 other events, 65.3 us)
Sparse Core Ops, SparseCore 0:
  173.8 111.0 all-reduce.4
  580.5 104.0 all-reduce.6
